TPU v7x, 32 devices: a whole 2x2x4 slice. The times are simulated.
32 devices in a mesh: row: 4 (over z), col: 4 (over y, core), rep: 2 (over x).
Axes of the slice: x: 2, y: 2, z: 4, core: 2. Of those that a mesh axis runs over, the one named last changes fastest.
Arguments:
- hamiltonian: bfloat16 [2048, 2048], P('row', ('rep', 'col')), may hold values from -0.21875 to 0.21875
- density: bfloat16 [2048, 2048], P(('rep', 'row'), 'col'), may hold values from -6 to 6
- ham_pattern: int32 [32, 32], P('row', ('rep', 'col')), may hold values 0 or 1
- den_pattern: int32 [32, 32], P(('rep', 'row'), 'col'), may hold values 0 or 1
- tile_basis: bfloat16 [64, 16, 512], P(None, None, 'col'), may hold values from -0.75 to 0.75
- offsets: int32 [32], P(('row', 'rep')), may hold values from 0 to 31
Outputs:
- product: bfloat16 [2048, 2048], P(('row', 'rep'), 'col')
- grid_density: float32 [256, 512], P(('row', 'rep'), 'col')
All inputs are finite; a program needn't handle non-finite values. No bound on the sum of `ham_pattern` or of `den_pattern` on one device may be relied on, other than what follows from the above.
Results may differ from a plain program's by a relative error of at most 0.0004.
Values may be sent and summed in bfloat16 or wider, within the bound.
A program may use at most 128 MiB of HBM per device.

v0:
```python
import math

import jax
import jax.numpy as jnp
from jax import lax
from jax.sharding import PartitionSpec as P

SX = 32
TX = 16


def shifted(value, axis, steps):
    count = lax.axis_size(axis)
    pairs = [(source, (source + steps) % count) for source in range(count)]
    return lax.ppermute(value, axis, pairs)


def expand(matrix, pattern):
    rows_b, cols_b = pattern.shape
    block = matrix.shape[0] // rows_b
    weight = pattern.astype(matrix.dtype)
    shaped = matrix.reshape(rows_b, block, cols_b, block) * weight[:, None, :, None]
    return shaped.reshape(matrix.shape)


def row_charges(full_rows):
    return lax.psum(jnp.sum(full_rows, axis=1), "col")


def shards(hamiltonian, density, ham_pattern, den_pattern, tile_basis, offsets):
    ham = expand(hamiltonian, ham_pattern)
    dens = expand(density, den_pattern)
    n_col = lax.axis_size("col")
    den_half = lax.all_gather(dens, "row", axis=0, tiled=True)
    partial_terms = jnp.dot(
        lax.all_gather(ham, "col", axis=1, tiled=True), den_half, preferred_element_type=jnp.float32
    )
    full_rows = lax.psum_scatter(partial_terms, "rep", scatter_dimension=0, tiled=True)
    sums = row_charges(full_rows)
    total_order = full_rows.shape[1] * n_col
    atoms = offsets.shape[0]
    amplitudes = (sums * (1.0 / math.sqrt(total_order))).reshape(atoms, -1)
    tiles = jnp.einsum(
        "am,mtp->atp", amplitudes, tile_basis.astype(jnp.float32), precision=lax.Precision.HIGHEST
    )
    planes = offsets[:, None] + jnp.arange(TX, dtype=jnp.int32)[None, :]
    onehot = (planes[:, :, None] == jnp.arange(SX + TX, dtype=jnp.int32)[None, None, :]).astype(
        jnp.float32
    )
    extended = jnp.einsum("atx,atp->xp", onehot, tiles, precision=lax.Precision.HIGHEST)
    own_planes = extended[:SX]
    incoming = shifted(extended[SX:], ("row", "rep"), 1)
    grid_density = jnp.concatenate([own_planes[:TX] + incoming, own_planes[TX:]], axis=0)
    return (full_rows.astype(jnp.bfloat16), grid_density)


def solution(mesh):
    in_specs = (
        P("row", ("rep", "col")),
        P(("rep", "row"), "col"),
        P("row", ("rep", "col")),
        P(("rep", "row"), "col"),
        P(None, None, "col"),
        P(("row", "rep")),
    )
    out_specs = (P(("row", "rep"), "col"), P(("row", "rep"), "col"))
    return jax.shard_map(shards, mesh=mesh, in_specs=in_specs, out_specs=out_specs, check_vma=False)
```

profile of v0, /device:TPU:0, one launch (start us, length us, event | category | flops | bytes accessed | tf_op | source)
XLA Modules:
  0.0 105.4 jit_solution(4507504190463637593)
XLA Ops:
  7.2 0.0 copy-start
  7.2 0.0 all-gather.3.cloned.1.call-start
  7.2 0.7 convert_element_type.11
  7.9 0.1 copy.8
  8.0 0.2 mul.28
  8.3 0.0 copy-start.1
  8.3 0.3 mul.29
  8.6 0.6 copy-done.1
  9.2 0.8 mul.30
  10.0 0.0 copy-start.3
  10.0 0.0 all-gather.3.cloned.1.call-update
  10.0 0.0 all-gather.5.cloned.1.call-start
  10.1 0.6 copy-done.3
  10.7 0.1 mul.31
  10.8 0.0 copy-start.2
  10.8 0.3 mul.32
  11.1 0.6 copy-done.2
  11.8 0.8 mul.33
  12.5 0.0 all-gather.5.cloned.1.call-update
  12.6 0.0 reduce-scatter.2.cloned.1.call-start
  12.6 17.1 %all-gather.3.cloned.1.call-done = bf16[512,1024]{1,0:T(8,128)(2,1)} async-done(((bf16[512,256]{1,0:T(8,128)(2,1)}), bf16[512,1024]{1,0:T(8,128)(2,1)}) %all-gather.3.cloned.1.call-update) | async-done | bytes 1048592 | tf_op jit(solution)/shard_map/all_gather | solution.py:36
  29.7 29.5 %all-gather.5.cloned.1.call-done = bf16[1024,512]{1,0:T(8,128)(2,1)} async-done(((bf16[256,512]{1,0:T(8,128)(2,1)}), bf16[1024,512]{1,0:T(8,128)(2,1)}) %all-gather.5.cloned.1.call-update) | async-done | bytes 1048592 | tf_op jit(solution)/shard_map/all_gather | solution.py:34
  59.3 3.2 %fusion.5 = f32[512,512]{1,0:T(8,128)} fusion(bf16[512,1024]{1,0:T(8,128)(2,1)} %all-gather.3.cloned.1.call-done, bf16[1024,512]{1,0:T(8,128)(2,1)} %all-gather.5.cloned.1.call-done), kind=kOutput, calls=%fused_computation.11 | convolution fusion | flops 536870912 | bytes 3145728 | tf_op jit(solution)/shard_map/dot_general | solution.py:35
  62.5 0.0 copy-start.4
  62.5 0.0 reduce-scatter.2.cloned.1.call-update
  62.5 0.6 copy-done.4
  63.1 0.1 iota_add_fusion
  63.2 19.2 %reduce-scatter.2.cloned.1.call-done = f32[256,512]{1,0:T(8,128)} async-done(((f32[512,512]{1,0:T(8,128)}), f32[256,512]{1,0:T(8,128)}) %reduce-scatter.2.cloned.1.call-update) | async-done | bytes 524304 | tf_op jit(solution)/shard_map/reduce_scatter | solution.py:38
  82.5 2.0 %fusion.4 = (f32[256]{0:T(256)S(1)}, bf16[256,512]{1,0:T(8,128)(2,1)}) fusion(f32[256,512]{1,0:T(8,128)} %reduce-scatter.2.cloned.1.call-done), kind=kLoop, calls=%fused_computation.10 | loop fusion | flops 261888 | bytes 787456 | tf_op jit(solution)/shard_map/reduce_sum | solution.py:27
  84.4 6.8 %psum.7 = f32[256]{0:T(256)S(1)} all-reduce(f32[256]{0:T(256)S(1)} %get-tuple-element.2), channel_id=1, replica_groups=mesh['row'=4,'col'=4,'rep'=2] {'col'}, use_global_device_ids=true, to_apply=%region_2.0 | all-reduce | flops 256 | bytes 2048 | tf_op jit(solution)/shard_map/psum | solution.py:27
  91.3 0.1 reshape.37
  91.4 0.0 copy-done
  91.4 0.2 fusion
  91.6 0.3 convolution_bitcast_fusion
  91.9 0.6 collective-permute-start
  92.5 5.8 %collective-permute-done = f32[16,128]{1,0:T(8,128)S(1)} collective-permute-done((f32[16,128]{1,0:T(8,128)S(1)}, f32[16,128]{1,0:T(8,128)S(1)}, u32[]{:S(2)}, u32[]{:S(2)}) %collective-permute-start) | collective-permute-done | bytes 8224 | tf_op jit(solution)/shard_map/ppermute | solution.py:15
  98.3 0.6 pad_maximum_fusion
  (4 shorter events, 0.0 us)
Async XLA Ops:
  7.2 84.2 %copy-start = (bf16[64,16,128]{2,1,0:T(8,128)(2,1)S(1)}, bf16[64,16,128]{2,1,0:T(8,128)(2,1)}, u32[]{:S(2)}) copy-start(bf16[64,16,128]{2,1,0:T(8,128)(2,1)} %param.10) | copy-start | bytes 786436
  7.2 22.5 %all-gather.3.cloned.1.call-start = ((), (), s32[]{:S(2)}) async-start(), calls=%async_computation.1 | async-start | bytes 1310720 | tf_op jit(solution)/shard_map/all_gather | solution.py:36
  8.3 1.0 copy-start.1
  10.0 0.7 copy-start.3
  10.0 49.3 %all-gather.5.cloned.1.call-start = ((), (), s32[]{:S(2)}) async-start(), calls=%async_computation.2 | async-start | bytes 1310720 | tf_op jit(solution)/shard_map/all_gather | solution.py:34
  10.8 1.0 copy-start.2
  12.6 69.9 %reduce-scatter.2.cloned.1.call-start = ((), (), s32[]{:S(2)}) async-start(), calls=%async_computation.3 | async-start | bytes 1572864 | tf_op jit(solution)/shard_map/reduce_scatter | solution.py:38
  62.5 0.7 copy-start.4
  91.9 6.4 %collective-permute-start = (f32[16,128]{1,0:T(8,128)S(1)}, f32[16,128]{1,0:T(8,128)S(1)}, u32[]{:S(2)}, u32[]{:S(2)}) collective-permute-start(f32[16,128]{1,0:T(8,128)S(1)} %slice.16), channel_id=1, source_target_pairs={{0,1},{1,8},{8,9},{9,16},{16,17},{17,24},{24,25},{25,0},{2,3},{3,1... | collective-permute-start | bytes 24584 | tf_op jit(solution)/shard_map/ppermute | solution.py:15
Sparse Core Ops, SparseCore 0:
  10.1 19.5 all-gather.2
  31.3 27.9 all-gather.4
  62.6 19.7 reduce-scatter.1
where the time goes:
time: 106 us; the launch traced here: 105 us
  waiting for transfers between devices  71.7 us (68%)
  between operations  13.8 us (13%)
  blocking collectives  6.84 us (6%)
  other arithmetic  4.92 us (5%)
  matrix products  3.74 us (4%)
  local copies, waits for them, and re-layouts  3.66 us (3%)
    all_gather x1, waiting for transfers between devices, shards(): den_half = lax.all_gather(dens, 'row', axis=0, tiled=True)  29.5 us
    reduce_scatter x1, waiting for transfers between devices, shards(): lax.psum_scatter(partial_terms, 'rep', scatter_dimension=0, tiled=True)  19.2 us
    all_gather x1, waiting for transfers between devices, shards(): lax.all_gather(ham, 'col', axis=1, tiled=True)  17.1 us
    psum x1, blocking collectives, row_charges(): return lax.psum(jnp.sum(full_rows, axis=1), 'col')  6.84 us
    ppermute x1, waiting for transfers between devices, shifted(): return lax.ppermute(value, axis, pairs)  5.76 us
    dot_general x1, matrix products, shards(): jnp.dot(lax.all_gather(ham, 'col', axis=1, tiled=True), den_half, preferr...  3.23 us
    unnamed x10, local copies, waits for them, and re-layouts  2.47 us
  transfers between devices with their start and end apart: 4, of which 4 were waited for; matrix products, arithmetic and copies ran while one was open for 1% of the time, Pallas kernels for 0%

commit v1 on v0

v1 whole, which is shorter than its diff:
```python
import functools
import math

import jax
import jax.numpy as jnp
from jax import lax
from jax.experimental import pallas as pl
from jax.experimental.pallas import tpu as pltpu
from jax.sharding import PartitionSpec as P

MESH = pl.DeviceIdType.MESH
TX = 16
LANES = 128
F32 = jnp.float32
BF16 = jnp.bfloat16
NT = (((1,), (1,)), ((), ()))


def flipped(index, mask):
    bit = 1
    while bit <= mask:
        if mask & bit:
            index = index + bit - 2 * bit * ((index // bit) % 2)
        bit *= 2
    return index


def low_bit(mask):
    return mask & -mask


def mask_row(pattern, row, width):
    blocks = pattern.shape[1]
    lane = lax.broadcasted_iota(jnp.int32, (1, width), 1) // (width // blocks)
    values = jnp.zeros((1, width), jnp.int32)
    for block in range(blocks):
        values = jnp.where(lane == block, pattern[row, block], values)
    return values.astype(F32).astype(BF16)


def kernel(
    R, C, ham, den, hpat, dpat, basis, offsets, out, grid,
    hbuf, dbuf, psend, pown, precv, scol, srow, tbuf, trecv, chcol, tiles, ext, incoming,
    hs, hr, drs, drr, dls, dlr, xs, xr, cs, cr, ws, wr, ts, tr, gs, gr,
):
    r, c, p = lax.axis_index("row"), lax.axis_index("col"), lax.axis_index("rep")
    MR, KH = ham.shape
    KD, W = den.shape
    MH, Q, KHALF = MR // 2, W // LANES, C * KH
    atoms = offsets.shape[0]
    block = MH // atoms
    sx = grid.shape[0]
    slab, slabs = r * 2 + p, R * 2
    after, before = (slab + 1) % slabs, (slab + slabs - 1) % slabs
    next_id = {"row": after // 2, "rep": after % 2}
    last_id = {"row": before // 2, "rep": before % 2}
    peer = {"rep": 1 - p}

    barrier = pltpu.get_barrier_semaphore()
    friends = [{"col": (c + k) % C} for k in range(1, C)] + [{"row": (r + k) % R} for k in range(1, R)]
    friends += [peer, next_id, last_id]
    for friend in friends:
        pl.semaphore_signal(barrier, inc=1, device_id=friend, device_id_type=MESH)

    def remote(src, dst, send, recv, to):
        return pltpu.make_async_remote_copy(
            src_ref=src, dst_ref=dst, send_sem=send, recv_sem=recv, device_id=to, device_id_type=MESH
        )

    def den_rows(q, owner):
        return dbuf.at[q, pl.ds(pl.multiple_of(owner * KD, KD), KD), :]

    def to_right(q, d):
        rows = den_rows(q, (r - d + R) % R)
        return remote(rows, rows, drs.at[q, d], drr.at[q, d + 1], {"row": (r + 1) % R})

    def to_left(q, d):
        rows = den_rows(q, (r + d) % R)
        return remote(rows, rows, dls.at[q, d], dlr.at[q, d + 1], {"row": (r + R - 1) % R})

    def send_right(q, d):
        @pl.when(jnp.logical_and(r - d >= 0, r + 1 < R))
        def _():
            to_right(q, d).start()

    def send_left(q, d):
        @pl.when(jnp.logical_and(r + d < R, r >= 1))
        def _():
            to_left(q, d).start()

    def own(q):
        send_right(q, 0)
        send_left(q, 0)

    def arrive(q, d):
        @pl.when(r - d >= 0)
        def _():
            rows = den_rows(q, (r - d + R) % R)
            remote(rows, rows, drs.at[q, d], drr.at[q, d], {"row": (r + 1) % R}).wait_recv()

        if d < R - 1:
            send_right(q, d)

        @pl.when(r + d < R)
        def _():
            rows = den_rows(q, (r + d) % R)
            remote(rows, rows, dls.at[q, d], dlr.at[q, d], {"row": (r + R - 1) % R}).wait_recv()

        if d < R - 1:
            send_left(q, d)

    bits = [1 << k for k in range(C.bit_length() - 1)]

    def ham_copy(mask, bit):
        source = hbuf.at[flipped(c, mask)]
        return remote(source, source, hs.at[mask, bit.bit_length() - 1], hr.at[mask | bit], {"col": flipped(c, bit)})

    def ham_forward(mask):
        for bit in reversed(bits):
            if mask == 0 or bit < low_bit(mask):
                ham_copy(mask, bit).start()

    def ham_arrive():
        for mask in sorted(range(1, C), key=lambda m: (-low_bit(m), m)):
            source = hbuf.at[flipped(c, mask)]
            remote(source, source, hs.at[mask, 0], hr.at[mask], {"col": flipped(c, 1)}).wait_recv()
            ham_forward(mask)

    dmasks = [mask_row(dpat, a, W) for a in range(dpat.shape[0])]
    tall = KD // dpat.shape[0]

    def mask_den(q):
        for a, values in enumerate(dmasks):
            rows = pl.ds(pl.multiple_of(r * KD + a * tall, tall), tall)
            dbuf[q, rows, :] = den[a * tall : (a + 1) * tall, q * LANES : (q + 1) * LANES] * values[:, q * LANES : (q + 1) * LANES]

    for q in range(Q):
        mask_den(q)
    high = MR // hpat.shape[0]
    for a in range(hpat.shape[0]):
        hbuf[c, a * high : (a + 1) * high, :] = ham[a * high : (a + 1) * high, :] * mask_row(hpat, a, KH)

    pl.semaphore_wait(barrier, len(friends))
    own(0)
    ham_forward(0)

    ones = jnp.ones((16, LANES), BF16)
    mine = jnp.zeros((16, KD), F32)
    for q in range(Q):
        mine += lax.dot_general(ones, den_rows(q, r)[...], NT, preferred_element_type=F32)
    scol[c] = mine[:8]

    def col_copy(k):
        return remote(scol.at[c], scol.at[c], cs.at[k], cr.at[k], {"col": (c + k) % C})

    for k in range(1, C):
        col_copy(k).start()
    if Q > 1:
        own(1)

    def row_copy(k):
        return remote(srow.at[r], srow.at[r], ws.at[k], wr.at[k], {"row": (r + k) % R})

    def sums_over_col():
        for k in range(1, C):
            source = scol.at[(c - k + C) % C]
            remote(source, source, cs.at[k], cr.at[k], {"col": (c + k) % C}).wait_recv()
        total = scol[0]
        for k in range(1, C):
            total += scol[k]
        srow[r] = total
        for k in range(1, R):
            row_copy(k).start()

    def t_copy():
        return remote(tbuf.at[1 - p], trecv, ts, tr, peer)

    def row_sums():
        for k in range(1, R):
            source = srow.at[(r - k + R) % R]
            remote(source, source, ws.at[k], wr.at[k], {"row": (r + k) % R}).wait_recv()
        step = min(KD, KH)
        total = jnp.zeros((24, MR), F32)
        for k in range(0, KHALF, step):
            piece = srow[k // KD, :, k % KD : k % KD + step]
            high_part = piece.astype(BF16).astype(F32)
            rest = piece - high_part
            mid_part = rest.astype(BF16).astype(F32)
            parts = jnp.concatenate([high_part, mid_part, rest - mid_part], axis=0).astype(BF16)
            total += lax.dot_general(
                parts, hbuf[k // KH, :, k % KH : k % KH + step], NT, preferred_element_type=F32
            )
        total = total[:8] + total[8:16] + total[16:]
        tbuf[0] = total[:, :MH]
        tbuf[1] = total[:, MH:]
        t_copy().start()

    def g_copy():
        return remote(ext.at[pl.ds(sx, TX), :], incoming, gs, gr, next_id)

    def collocate():
        t_copy().wait_recv()
        charges = (tbuf[p, 0:1, :] + trecv[0:1, :]) * (1.0 / math.sqrt(KHALF * 2))
        chcol[...] = jnp.transpose(jnp.broadcast_to(charges, (LANES, MH)))

        def body(m, sums):
            values = basis[m].astype(F32)
            return tuple(s + values * chcol[pl.ds(a * block + m, 1), :] for a, s in enumerate(sums))

        zero = jnp.zeros((TX, grid.shape[1]), F32)
        sums = lax.fori_loop(0, block, body, (zero,) * atoms, unroll=4)
        for a in range(atoms):
            tiles[a * TX : (a + 1) * TX, :] = sums[a]
        place = lax.broadcasted_iota(jnp.int32, (1, atoms * TX), 1)
        first = jnp.zeros((1, atoms * TX), jnp.int32)
        for a in range(atoms):
            first = jnp.where(place // TX == a, offsets[a], first)
        plane = lax.broadcasted_iota(jnp.int32, (sx + TX, atoms * TX), 0)
        onehot = jnp.where(plane == first + place % TX, 1.0, 0.0).astype(F32)
        ext[...] = jnp.dot(onehot, tiles[...], precision=lax.Precision.HIGHEST, preferred_element_type=F32)
        g_copy().start()

    def finish_grid():
        g_copy().wait_recv()
        grid[...] = ext[:sx, :]
        grid[:TX, :] = ext[:TX, :] + incoming[...]

    def x_copy(q):
        return remote(psend.at[q], precv.at[q], xs.at[q], xr.at[q], peer)

    def half(q, which):
        rows = pl.ds(pl.multiple_of(which * MH, MH), MH)
        total = jnp.zeros((MH, LANES), F32)
        for j in range(C):
            total += jnp.dot(hbuf[j, rows, :], dbuf[q, j * KH : (j + 1) * KH, :], preferred_element_type=F32)
        return total

    def multiply(q):
        psend[q] = half(q, 1 - p)
        x_copy(q).start()
        pown[q] = half(q, p)

    def drain(q):
        x_copy(q).wait_recv()
        out[:, q * LANES : (q + 1) * LANES] = (pown[q] + precv[q]).astype(BF16)

    hooks = {
        (0, 1): [sums_over_col],
        (0, R - 1): [ham_arrive],
        (1, 1): [row_sums, lambda: multiply(0)],
        (1, R - 1): [lambda: multiply(1)],
        (2, 1): [collocate],
        (2, R - 1): [lambda: multiply(2), lambda: drain(0)],
        (3, 1): [finish_grid, lambda: drain(1)],
        (3, R - 1): [lambda: multiply(3), lambda: drain(2), lambda: drain(3)],
    }
    for q in range(Q):
        for d in range(1, R):
            arrive(q, d)
            if d == R - 1 and q + 2 < Q:
                own(q + 2)
            for hook in hooks.get((q, d), []):
                hook()

    for q in range(Q):
        x_copy(q).wait_send()
        for d in range(R - 1):
            @pl.when(jnp.logical_and(r - d >= 0, r + 1 < R))
            def _():
                to_right(q, d).wait_send()

            @pl.when(jnp.logical_and(r + d < R, r >= 1))
            def _():
                to_left(q, d).wait_send()

    for mask in range(C):
        for bit in bits:
            if mask == 0 or bit < low_bit(mask):
                ham_copy(mask, bit).wait_send()
    for k in range(1, C):
        col_copy(k).wait_send()
    for k in range(1, R):
        row_copy(k).wait_send()
    t_copy().wait_send()
    g_copy().wait_send()


def shards(R, C, hamiltonian, density, ham_pattern, den_pattern, tile_basis, offsets):
    MR, KH = hamiltonian.shape
    KD, W = density.shape
    MH, Q, KHALF = MR // 2, W // LANES, C * KH
    cells, atoms = tile_basis.shape[2], offsets.shape[0]
    sx = 32
    dma = pltpu.SemaphoreType.DMA
    vmem = pl.BlockSpec(memory_space=pltpu.VMEM)
    smem = pl.BlockSpec(memory_space=pltpu.SMEM)
    return pl.pallas_call(
        functools.partial(kernel, R, C),
        out_shape=(jax.ShapeDtypeStruct((MH, W), BF16), jax.ShapeDtypeStruct((sx, cells), F32)),
        in_specs=[vmem, vmem, smem, smem, vmem, smem],
        out_specs=(vmem, vmem),
        scratch_shapes=[
            pltpu.VMEM((C, MR, KH), BF16),
            pltpu.VMEM((Q, KHALF, LANES), BF16),
            pltpu.VMEM((Q, MH, LANES), F32),
            pltpu.VMEM((Q, MH, LANES), F32),
            pltpu.VMEM((Q, MH, LANES), F32),
            pltpu.VMEM((C, 8, KD), F32),
            pltpu.VMEM((R, 8, KD), F32),
            pltpu.VMEM((2, 8, MH), F32),
            pltpu.VMEM((8, MH), F32),
            pltpu.VMEM((MH, LANES), F32),
            pltpu.VMEM((atoms * TX, cells), F32),
            pltpu.VMEM((sx + TX, cells), F32),
            pltpu.VMEM((TX, cells), F32),
            dma((C, C.bit_length())),
            dma((C,)),
            dma((Q, R)),
            dma((Q, R)),
            dma((Q, R)),
            dma((Q, R)),
            dma((Q,)),
            dma((Q,)),
            dma((C,)),
            dma((C,)),
            dma((R,)),
            dma((R,)),
            dma,
            dma,
            dma,
            dma,
        ],
        compiler_params=pltpu.CompilerParams(
            collective_id=0, has_side_effects=True, vmem_limit_bytes=40 * 1024 * 1024
        ),
    )(hamiltonian, density, ham_pattern, den_pattern, tile_basis, offsets)


def solution(mesh):
    in_specs = (
        P("row", ("rep", "col")),
        P(("rep", "row"), "col"),
        P("row", ("rep", "col")),
        P(("rep", "row"), "col"),
        P(None, None, "col"),
        P(("row", "rep")),
    )
    out_specs = (P(("row", "rep"), "col"), P(("row", "rep"), "col"))
    body = functools.partial(shards, mesh.shape["row"], mesh.shape["col"])
    return jax.shard_map(body, mesh=mesh, in_specs=in_specs, out_specs=out_specs, check_vma=False)
```

time: 106 us -> 43.9 us (0.41)
  waiting for transfers between devices: 71.7 us -> 0 us
  Pallas kernels: 0 us -> 38.1 us
  between operations: 13.8 us -> 0.66 us
  blocking collectives: 6.84 us -> 0 us
  other arithmetic: 4.92 us -> 0 us
  matrix products: 3.74 us -> 0 us
  local copies, waits for them, and re-layouts: 3.66 us -> 4.94 us
    all_gather x2 -> x0, waiting for transfers between devices: 46.6 us -> none  [the longest x1 29.5 us: shards(): den_half = lax.all_gather(dens, 'row', axis=0, tiled=True)]
    pallas_call x0 -> x1, Pallas kernels: none -> 38.1 us  [shards(): pl.pallas_call(functools.partial(kernel, R, C), out_shape=(jax.ShapeDtype...]
    reduce_scatter x1 -> x0, waiting for transfers between devices: 19.2 us -> none  [shards(): lax.psum_scatter(partial_terms, 'rep', scatter_dimension=0, tiled=True)]
    psum x1 -> x0, blocking collectives: 6.84 us -> none  [row_charges(): return lax.psum(jnp.sum(full_rows, axis=1), 'col')]
    ppermute x1 -> x0, waiting for transfers between devices: 5.76 us -> none  [shifted(): return lax.ppermute(value, axis, pairs)]
    dot_general x3 -> x0, matrix products: 3.74 us -> none  [the longest x1 3.23 us: shards(): jnp.dot(lax.all_gather(ham, 'col', axis=1, tiled=True), den_half, preferr...]
    unnamed x10 -> x13, local copies, waits for them, and re-layouts: 2.47 us -> 4.94 us
    reduce_sum x1 -> x0, other arithmetic: 1.97 us -> none  [row_charges(): return lax.psum(jnp.sum(full_rows, axis=1), 'col')]
  transfers between devices with their start and end apart: 4 -> 0, of which waited for: 4 -> 0; matrix products, arithmetic and copies ran while one was open for 1% -> 0% of each run, Pallas kernels for 0% -> 0%
where the time goes in v1:
time: 43.9 us; the launch traced here: 43.7 us
  Pallas kernels  38.1 us (87%)
  local copies, waits for them, and re-layouts  4.94 us (11%)
  between operations  0.66 us (2%)
    pallas_call x1, Pallas kernels, shards(): pl.pallas_call(functools.partial(kernel, R, C), out_shape=(jax.ShapeDtype...  38.1 us
    unnamed x13, local copies, waits for them, and re-layouts  4.94 us

profile of v1, /device:TPU:0, one launch (start us, length us, event | category | flops | bytes accessed | tf_op | source)
XLA Modules:
  0.0 43.7 jit_solution(6448312832951981061)
XLA Ops:
  0.6 0.0 copy-start.4
  0.6 0.0 copy-start.3
  0.7 0.8 %copy.8.hpat = s32[8,4]{1,0:T(8,128)S(1)} copy(s32[8,4]{0,1:T(4,128)} %param.8) | data formatting | bytes 256 | tf_op args[2]
  1.4 0.0 copy-done.4
  1.4 0.0 copy-done.3
  1.4 0.0 copy-start
  1.4 0.9 %copy-done = bf16[512,256]{1,0:T(8,128)(2,1)S(1)} copy-done((bf16[512,256]{1,0:T(8,128)(2,1)S(1)}, bf16[512,256]{1,0:T(8,128)(2,1)}, u32[]{:S(2)}) %copy-start) | copy-done | bytes 262168
  2.4 0.0 copy-start.1
  2.4 0.9 %copy-done.1 = bf16[256,512]{1,0:T(8,128)(2,1)S(1)} copy-done((bf16[256,512]{1,0:T(8,128)(2,1)S(1)}, bf16[256,512]{1,0:T(8,128)(2,1)}, u32[]{:S(2)}) %copy-start.1) | copy-done | bytes 262168
  3.3 0.0 copy-start.2
  3.3 0.9 %copy-done.2 = bf16[64,16,128]{2,1,0:T(8,128)(2,1)S(1)} copy-done((bf16[64,16,128]{2,1,0:T(8,128)(2,1)S(1)}, bf16[64,16,128]{2,1,0:T(8,128)(2,1)}, u32[]{:S(2)}) %copy-start.2) | copy-done | bytes 262168
  4.3 38.1 %shard_map.77 = (bf16[256,512]{1,0:T(8,128)(2,1)S(1)}, f32[32,128]{1,0:T(8,128)S(1)}) custom-call(bf16[512,256]{1,0:T(8,128)(2,1)S(1)} %copy-done, bf16[256,512]{1,0:T(8,128)(2,1)S(1)} %copy-done.1, s32[8,4]{1,0:T(8,128)S(1)} %copy.8.hpat, s32[4,8]{1,0:T(4,128)S(1)} %copy-done.3, bf16[64,16,128]{2,1,0:T(8,128)(2,1)S(1)} %copy-done.2, s32[4]{0:T(128)S(1)} %copy-done.4), custom_call_target="tpu_custom_call" | custom-call | tf_op jit(solution)/shard_map/pallas_call | solution.py:297
  42.4 0.7 %copy.11 = bf16[256,512]{1,0:T(8,128)(2,1)} copy(bf16[256,512]{1,0:T(8,128)(2,1)S(1)} %get-tuple-element.4) | data formatting | bytes 524288
  43.1 0.6 %copy.12 = f32[32,128]{1,0:T(8,128)} copy(f32[32,128]{1,0:T(8,128)S(1)} %get-tuple-element.5) | data formatting | bytes 32768
Async XLA Ops:
  0.6 0.8 %copy-start.4 = (s32[4]{0:T(128)S(1)}, s32[4]{0:T(128)}, u32[]{:S(2)}) copy-start(s32[4]{0:T(128)} %offsets.1) | copy-start | bytes 52
  0.6 0.8 %copy-start.3 = (s32[4,8]{1,0:T(4,128)S(1)}, s32[4,8]{1,0:T(4,128)}, u32[]{:S(2)}) copy-start(s32[4,8]{1,0:T(4,128)} %dpat.1) | copy-start | bytes 388
  1.4 1.0 %copy-start = (bf16[512,256]{1,0:T(8,128)(2,1)S(1)}, bf16[512,256]{1,0:T(8,128)(2,1)}, u32[]{:S(2)}) copy-start(bf16[512,256]{1,0:T(8,128)(2,1)} %ham.1) | copy-start | bytes 786436
  2.4 0.9 %copy-start.1 = (bf16[256,512]{1,0:T(8,128)(2,1)S(1)}, bf16[256,512]{1,0:T(8,128)(2,1)}, u32[]{:S(2)}) copy-start(bf16[256,512]{1,0:T(8,128)(2,1)} %den.1) | copy-start | bytes 786436
  3.3 0.9 %copy-start.2 = (bf16[64,16,128]{2,1,0:T(8,128)(2,1)S(1)}, bf16[64,16,128]{2,1,0:T(8,128)(2,1)}, u32[]{:S(2)}) copy-start(bf16[64,16,128]{2,1,0:T(8,128)(2,1)} %basis.1) | copy-start | bytes 786436

commit v2 on v1

--- a/solution.py
+++ b/solution.py
@@ -11,6 +11,7 @@
 MESH = pl.DeviceIdType.MESH
 TX = 16
 LANES = 128
+VMEM_MIB = 63
 F32 = jnp.float32
 BF16 = jnp.bfloat16
 NT = (((1,), (1,)), ((), ()))
@@ -29,19 +30,19 @@
     return mask & -mask
 
 
-def mask_row(pattern, row, width):
-    blocks = pattern.shape[1]
+def mask_row(pick, blocks, row, width):
     lane = lax.broadcasted_iota(jnp.int32, (1, width), 1) // (width // blocks)
     values = jnp.zeros((1, width), jnp.int32)
     for block in range(blocks):
-        values = jnp.where(lane == block, pattern[row, block], values)
+        values = jnp.where(lane == block, pick(row, block), values)
     return values.astype(F32).astype(BF16)
 
 
 def kernel(
-    R, C, ham, den, hpat, dpat, basis, offsets, out, grid,
-    hbuf, dbuf, psend, pown, precv, scol, srow, tbuf, trecv, chcol, tiles, ext, incoming,
-    hs, hr, drs, drr, dls, dlr, xs, xr, cs, cr, ws, wr, ts, tr, gs, gr,
+    R, C, ham_in, den_in, hpat_in, dpat_in, basis_in, offsets_in, out, grid,
+    ham, den, hpat, dpat, basis, offsets,
+    hbuf, dbuf, psend, pown, precv, ssend, srecv, srow, tbuf, trecv, chcol, tiles, ext, incoming,
+    hs, hr, drs, drr, dls, dlr, xs, xr, cs, cr, ws, wr, ts, tr, gs, gr, loaded, hello,
 ):
     r, c, p = lax.axis_index("row"), lax.axis_index("col"), lax.axis_index("rep")
     MR, KH = ham.shape
@@ -56,11 +57,24 @@
     last_id = {"row": before // 2, "rep": before % 2}
     peer = {"rep": 1 - p}
 
+    bits = [1 << k for k in range(C.bit_length() - 1)]
+    even = c % 2 == 0
+    partner = {"col": flipped(c, 1)}
+
     barrier = pltpu.get_barrier_semaphore()
-    friends = [{"col": (c + k) % C} for k in range(1, C)] + [{"row": (r + k) % R} for k in range(1, R)]
+    friends = [{"row": (r + k) % R} for k in range(1, R)] + [{"col": flipped(c, bit)} for bit in bits[1:]]
     friends += [peer, next_id, last_id]
     for friend in friends:
         pl.semaphore_signal(barrier, inc=1, device_id=friend, device_id_type=MESH)
+
+    @pl.when(even)
+    def _():
+        pl.semaphore_signal(barrier, inc=1, device_id=partner, device_id_type=MESH)
+
+    pairs = [(dpat_in, dpat), (den_in, den), (hpat_in, hpat), (ham_in, ham), (basis_in, basis), (offsets_in, offsets)]
+    loads = [pltpu.make_async_copy(a, b, loaded.at[k]) for k, (a, b) in enumerate(pairs)]
+    for load in loads:
+        load.start()
 
     def remote(src, dst, send, recv, to):
         return pltpu.make_async_remote_copy(
@@ -109,15 +123,13 @@
         if d < R - 1:
             send_left(q, d)
 
-    bits = [1 << k for k in range(C.bit_length() - 1)]
-
     def ham_copy(mask, bit):
         source = hbuf.at[flipped(c, mask)]
         return remote(source, source, hs.at[mask, bit.bit_length() - 1], hr.at[mask | bit], {"col": flipped(c, bit)})
 
     def ham_forward(mask):
         for bit in reversed(bits):
-            if mask == 0 or bit < low_bit(mask):
+            if bit < low_bit(mask):
                 ham_copy(mask, bit).start()
 
     def ham_arrive():
@@ -126,7 +138,9 @@
             remote(source, source, hs.at[mask, 0], hr.at[mask], {"col": flipped(c, 1)}).wait_recv()
             ham_forward(mask)
 
-    dmasks = [mask_row(dpat, a, W) for a in range(dpat.shape[0])]
+    loads[0].wait()
+    loads[1].wait()
+    dmasks = [mask_row(lambda i, j: dpat[i, j], dpat.shape[1], a, W) for a in range(dpat.shape[0])]
     tall = KD // dpat.shape[0]
 
     def mask_den(q):
@@ -134,41 +148,72 @@
             rows = pl.ds(pl.multiple_of(r * KD + a * tall, tall), tall)
             dbuf[q, rows, :] = den[a * tall : (a + 1) * tall, q * LANES : (q + 1) * LANES] * values[:, q * LANES : (q + 1) * LANES]
 
-    for q in range(Q):
+    def mask_ham():
+        high = MR // hpat.shape[1]
+        for a in range(hpat.shape[1]):
+            hbuf[c, a * high : (a + 1) * high, :] = ham[a * high : (a + 1) * high, :] * mask_row(lambda i, j: hpat[j, i], hpat.shape[0], a, KH)
+
+    mask_den(0)
+    loads[2].wait()
+    loads[3].wait()
+    mask_ham()
+
+    @pl.when(even)
+    def _():
+        pl.semaphore_wait(barrier, len(friends))
+
+    @pl.when(jnp.logical_not(even))
+    def _():
+        pl.semaphore_wait(barrier, len(friends) + 1)
+
+    own(0)
+    for bit in bits[1:]:
+        ham_copy(0, bit).start()
+
+    @pl.when(jnp.logical_not(even))
+    def _():
+        pl.semaphore_signal(hello, inc=1, device_id=partner, device_id_type=MESH)
+
+    for q in range(1, Q):
         mask_den(q)
-    high = MR // hpat.shape[0]
-    for a in range(hpat.shape[0]):
-        hbuf[c, a * high : (a + 1) * high, :] = ham[a * high : (a + 1) * high, :] * mask_row(hpat, a, KH)
-
-    pl.semaphore_wait(barrier, len(friends))
-    own(0)
-    ham_forward(0)
+        if q == 1:
+            own(1)
 
     ones = jnp.ones((16, LANES), BF16)
     mine = jnp.zeros((16, KD), F32)
     for q in range(Q):
         mine += lax.dot_general(ones, den_rows(q, r)[...], NT, preferred_element_type=F32)
-    scol[c] = mine[:8]
-
-    def col_copy(k):
-        return remote(scol.at[c], scol.at[c], cs.at[k], cr.at[k], {"col": (c + k) % C})
-
-    for k in range(1, C):
-        col_copy(k).start()
-    if Q > 1:
-        own(1)
+    ssend[len(bits) - 1] = mine[:8]
+
+    def s_copy(k):
+        return remote(ssend.at[k], srecv.at[k], cs.at[k], cr.at[k], {"col": flipped(c, bits[k])})
+
+    for load in loads[4:]:
+        load.wait()
+    if len(bits) > 1:
+        s_copy(len(bits) - 1).start()
 
     def row_copy(k):
         return remote(srow.at[r], srow.at[r], ws.at[k], wr.at[k], {"row": (r + k) % R})
 
-    def sums_over_col():
-        for k in range(1, C):
-            source = scol.at[(c - k + C) % C]
-            remote(source, source, cs.at[k], cr.at[k], {"col": (c + k) % C}).wait_recv()
-        total = scol[0]
-        for k in range(1, C):
-            total += scol[k]
-        srow[r] = total
+    def sums_over_chips():
+        for k in range(len(bits) - 1, 0, -1):
+            s_copy(k).wait_recv()
+            ssend[k - 1] = ssend[k] + srecv[k]
+            if k > 1:
+                s_copy(k - 1).start()
+
+    def meet_partner():
+        @pl.when(even)
+        def _():
+            pl.semaphore_wait(hello, 1)
+
+        ham_copy(0, 1).start()
+        s_copy(0).start()
+
+    def sums_over_cores():
+        s_copy(0).wait_recv()
+        srow[r] = ssend[0] + srecv[0]
         for k in range(1, R):
             row_copy(k).start()
 
@@ -245,8 +290,8 @@
         out[:, q * LANES : (q + 1) * LANES] = (pown[q] + precv[q]).astype(BF16)
 
     hooks = {
-        (0, 1): [sums_over_col],
-        (0, R - 1): [ham_arrive],
+        (0, 1): [sums_over_chips],
+        (0, R - 1): [meet_partner, ham_arrive, sums_over_cores],
         (1, 1): [row_sums, lambda: multiply(0)],
         (1, R - 1): [lambda: multiply(1)],
         (2, 1): [collocate],
@@ -277,8 +322,8 @@
         for bit in bits:
             if mask == 0 or bit < low_bit(mask):
                 ham_copy(mask, bit).wait_send()
-    for k in range(1, C):
-        col_copy(k).wait_send()
+    for k in range(len(bits)):
+        s_copy(k).wait_send()
     for k in range(1, R):
         row_copy(k).wait_send()
     t_copy().wait_send()
@@ -293,19 +338,26 @@
     sx = 32
     dma = pltpu.SemaphoreType.DMA
     vmem = pl.BlockSpec(memory_space=pltpu.VMEM)
-    smem = pl.BlockSpec(memory_space=pltpu.SMEM)
+    hbm = pl.BlockSpec(memory_space=pltpu.HBM)
     return pl.pallas_call(
         functools.partial(kernel, R, C),
         out_shape=(jax.ShapeDtypeStruct((MH, W), BF16), jax.ShapeDtypeStruct((sx, cells), F32)),
-        in_specs=[vmem, vmem, smem, smem, vmem, smem],
+        in_specs=[hbm] * 6,
         out_specs=(vmem, vmem),
         scratch_shapes=[
+            pltpu.VMEM((MR, KH), BF16),
+            pltpu.VMEM((KD, W), BF16),
+            pltpu.SMEM(ham_pattern.shape[::-1], jnp.int32),
+            pltpu.SMEM(den_pattern.shape, jnp.int32),
+            pltpu.VMEM(tile_basis.shape, BF16),
+            pltpu.SMEM(offsets.shape, jnp.int32),
             pltpu.VMEM((C, MR, KH), BF16),
             pltpu.VMEM((Q, KHALF, LANES), BF16),
             pltpu.VMEM((Q, MH, LANES), F32),
             pltpu.VMEM((Q, MH, LANES), F32),
             pltpu.VMEM((Q, MH, LANES), F32),
-            pltpu.VMEM((C, 8, KD), F32),
+            pltpu.VMEM((C.bit_length(), 8, KD), F32),
+            pltpu.VMEM((C.bit_length(), 8, KD), F32),
             pltpu.VMEM((R, 8, KD), F32),
             pltpu.VMEM((2, 8, MH), F32),
             pltpu.VMEM((8, MH), F32),
@@ -321,19 +373,21 @@
             dma((Q, R)),
             dma((Q,)),
             dma((Q,)),
-            dma((C,)),
-            dma((C,)),
+            dma((C.bit_length(),)),
+            dma((C.bit_length(),)),
             dma((R,)),
             dma((R,)),
             dma,
             dma,
             dma,
             dma,
+            dma((6,)),
+            pltpu.SemaphoreType.REGULAR,
         ],
         compiler_params=pltpu.CompilerParams(
-            collective_id=0, has_side_effects=True, vmem_limit_bytes=40 * 1024 * 1024
+            collective_id=0, has_side_effects=True, vmem_limit_bytes=VMEM_MIB * 1024 * 1024
         ),
-    )(hamiltonian, density, ham_pattern, den_pattern, tile_basis, offsets)
+    )(hamiltonian, density, ham_pattern.T, den_pattern, tile_basis, offsets)
 
 
 def solution(mesh):

time: 43.9 us -> 44.2 us (level)
  Pallas kernels: 38.1 us -> 41.1 us
  local copies, waits for them, and re-layouts: 4.94 us -> 2.28 us
    pallas_call x1, Pallas kernels: 38.1 us -> 41.1 us  [shards(): pl.pallas_call(functools.partial(kernel, R, C), out_shape=(jax.ShapeDtype...]
    unnamed x13 -> x4, local copies, waits for them, and re-layouts: 4.94 us -> 2.28 us
where the time goes in v2:
time: 44.2 us; the launch traced here: 44 us
  Pallas kernels  41.1 us (93%)
  local copies, waits for them, and re-layouts  2.28 us (5%)
  between operations  0.65 us (1%)
    pallas_call x1, Pallas kernels, shards(): pl.pallas_call(functools.partial(kernel, R, C), out_shape=(jax.ShapeDtype...  41.1 us
    unnamed x4, local copies, waits for them, and re-layouts  2.28 us

profile of v2, /device:TPU:0, one launch (start us, length us, event | category | flops | bytes accessed | tf_op | source)
XLA Modules:
  0.0 44.0 jit_solution(18251760474003272968)
XLA Ops:
  0.6 41.1 %shard_map.77 = (bf16[256,512]{1,0:T(8,128)(2,1)}, f32[32,128]{1,0:T(8,128)}) custom-call(bf16[512,256]{1,0:T(8,128)(2,1)} %ham_in.1, bf16[256,512]{1,0:T(8,128)(2,1)} %den_in.1, s32[4,8]{1,0:T(4,128)} %bitcast.1, s32[4,8]{1,0:T(4,128)} %dpat_in.1, bf16[64,16,128]{2,1,0:T(8,128)(2,1)} %basis_in.1, s32[4]{0:T(128)} %offsets_in.1), custom_call_target="tpu_custom_call" | custom-call | tf_op jit(solution)/shard_map/pallas_call | solution.py:342
  41.7 0.0 copy-start
  41.8 1.7 %copy.10 = bf16[256,512]{1,0:T(8,128)(2,1)} copy(bf16[256,512]{1,0:T(8,128)(2,1)} %get-tuple-element.4) | data formatting | bytes 524288
  43.4 0.0 copy-done
  43.4 0.6 %copy.11 = f32[32,128]{1,0:T(8,128)} copy(f32[32,128]{1,0:T(8,128)S(1)} %copy-done) | data formatting | bytes 32768
Async XLA Ops:
  41.7 1.7 %copy-start = (f32[32,128]{1,0:T(8,128)S(1)}, f32[32,128]{1,0:T(8,128)}, u32[]{:S(2)}) copy-start(f32[32,128]{1,0:T(8,128)} %get-tuple-element.5) | copy-start | bytes 49156

commit v3 on v2

--- a/solution.py
+++ b/solution.py
@@ -41,7 +41,7 @@
 def kernel(
     R, C, ham_in, den_in, hpat_in, dpat_in, basis_in, offsets_in, out, grid,
     ham, den, hpat, dpat, basis, offsets,
-    hbuf, dbuf, psend, pown, precv, ssend, srecv, srow, tbuf, trecv, chcol, tiles, ext, incoming,
+    hbuf, dbuf, psend, pown, precv, ssend, srecv, srow, tbuf, trecv, chcol, tiles, ext, incoming, done, stored,
     hs, hr, drs, drr, dls, dlr, xs, xr, cs, cr, ws, wr, ts, tr, gs, gr, loaded, hello,
 ):
     r, c, p = lax.axis_index("row"), lax.axis_index("col"), lax.axis_index("rep")
@@ -153,31 +153,8 @@
         for a in range(hpat.shape[1]):
             hbuf[c, a * high : (a + 1) * high, :] = ham[a * high : (a + 1) * high, :] * mask_row(lambda i, j: hpat[j, i], hpat.shape[0], a, KH)
 
-    mask_den(0)
-    loads[2].wait()
-    loads[3].wait()
-    mask_ham()
-
-    @pl.when(even)
-    def _():
-        pl.semaphore_wait(barrier, len(friends))
-
-    @pl.when(jnp.logical_not(even))
-    def _():
-        pl.semaphore_wait(barrier, len(friends) + 1)
-
-    own(0)
-    for bit in bits[1:]:
-        ham_copy(0, bit).start()
-
-    @pl.when(jnp.logical_not(even))
-    def _():
-        pl.semaphore_signal(hello, inc=1, device_id=partner, device_id_type=MESH)
-
-    for q in range(1, Q):
+    for q in range(Q):
         mask_den(q)
-        if q == 1:
-            own(1)
 
     ones = jnp.ones((16, LANES), BF16)
     mine = jnp.zeros((16, KD), F32)
@@ -188,10 +165,31 @@
     def s_copy(k):
         return remote(ssend.at[k], srecv.at[k], cs.at[k], cr.at[k], {"col": flipped(c, bits[k])})
 
+    loads[2].wait()
+    loads[3].wait()
+    mask_ham()
+
+    @pl.when(even)
+    def _():
+        pl.semaphore_wait(barrier, len(friends))
+
+    @pl.when(jnp.logical_not(even))
+    def _():
+        pl.semaphore_wait(barrier, len(friends) + 1)
+
+    if len(bits) > 1:
+        s_copy(len(bits) - 1).start()
+    for q in range(min(3, Q)):
+        own(q)
+    for bit in bits[1:]:
+        ham_copy(0, bit).start()
+
+    @pl.when(jnp.logical_not(even))
+    def _():
+        pl.semaphore_signal(hello, inc=1, device_id=partner, device_id_type=MESH)
+
     for load in loads[4:]:
         load.wait()
-    if len(bits) > 1:
-        s_copy(len(bits) - 1).start()
 
     def row_copy(k):
         return remote(srow.at[r], srow.at[r], ws.at[k], wr.at[k], {"row": (r + k) % R})
@@ -267,8 +265,8 @@
 
     def finish_grid():
         g_copy().wait_recv()
-        grid[...] = ext[:sx, :]
-        grid[:TX, :] = ext[:TX, :] + incoming[...]
+        ext[:TX, :] = ext[:TX, :] + incoming[...]
+        grid_copy().start()
 
     def x_copy(q):
         return remote(psend.at[q], precv.at[q], xs.at[q], xr.at[q], peer)
@@ -285,27 +283,35 @@
         x_copy(q).start()
         pown[q] = half(q, p)
 
+    def out_copy(q):
+        return pltpu.make_async_copy(done.at[q], out.at[:, pl.ds(q * LANES, LANES)], stored.at[q])
+
+    def grid_copy():
+        return pltpu.make_async_copy(ext.at[pl.ds(0, sx), :], grid, stored.at[Q])
+
     def drain(q):
         x_copy(q).wait_recv()
-        out[:, q * LANES : (q + 1) * LANES] = (pown[q] + precv[q]).astype(BF16)
+        done[q] = (pown[q] + precv[q]).astype(BF16)
+        out_copy(q).start()
 
     hooks = {
-        (0, 1): [sums_over_chips],
-        (0, R - 1): [meet_partner, ham_arrive, sums_over_cores],
-        (1, 1): [row_sums, lambda: multiply(0)],
-        (1, R - 1): [lambda: multiply(1)],
-        (2, 1): [collocate],
-        (2, R - 1): [lambda: multiply(2), lambda: drain(0)],
-        (3, 1): [finish_grid, lambda: drain(1)],
+        (0, 1): [sums_over_chips, meet_partner],
+        (1, 1): [sums_over_cores],
+        (0, 2): [ham_arrive],
+        (0, R - 1): [lambda: multiply(0)],
+        (2, 1): [row_sums],
+        (1, R - 1): [lambda: multiply(1), collocate],
+        (2, R - 1): [lambda: multiply(2), lambda: drain(0), finish_grid],
+        (3, R - 2): [lambda: drain(1)],
         (3, R - 1): [lambda: multiply(3), lambda: drain(2), lambda: drain(3)],
     }
-    for q in range(Q):
-        for d in range(1, R):
-            arrive(q, d)
-            if d == R - 1 and q + 2 < Q:
-                own(q + 2)
-            for hook in hooks.get((q, d), []):
-                hook()
+    steps = [(q, d) for q in range(Q) for d in range(1, R)]
+    for q, d in sorted(steps, key=lambda step: (step[0] + (step[1] > 1), step[1] > 1, step[1])):
+        arrive(q, d)
+        if d == 1 and q >= 1 and q + 2 < Q:
+            own(q + 2)
+        for hook in hooks.get((q, d), []):
+            hook()
 
     for q in range(Q):
         x_copy(q).wait_send()
@@ -328,6 +334,17 @@
         row_copy(k).wait_send()
     t_copy().wait_send()
     g_copy().wait_send()
+    for q in range(Q):
+        out_copy(q).wait()
+    grid_copy().wait()
+
+
+def hand_on(product, planes, out, grid, sems):
+    copies = [pltpu.make_async_copy(product, out, sems.at[0]), pltpu.make_async_copy(planes, grid, sems.at[1])]
+    for copy in copies:
+        copy.start()
+    for copy in copies:
+        copy.wait()
 
 
 def shards(R, C, hamiltonian, density, ham_pattern, den_pattern, tile_basis, offsets):
@@ -337,13 +354,12 @@
     cells, atoms = tile_basis.shape[2], offsets.shape[0]
     sx = 32
     dma = pltpu.SemaphoreType.DMA
-    vmem = pl.BlockSpec(memory_space=pltpu.VMEM)
     hbm = pl.BlockSpec(memory_space=pltpu.HBM)
-    return pl.pallas_call(
+    results = pl.pallas_call(
         functools.partial(kernel, R, C),
         out_shape=(jax.ShapeDtypeStruct((MH, W), BF16), jax.ShapeDtypeStruct((sx, cells), F32)),
         in_specs=[hbm] * 6,
-        out_specs=(vmem, vmem),
+        out_specs=(hbm, hbm),
         scratch_shapes=[
             pltpu.VMEM((MR, KH), BF16),
             pltpu.VMEM((KD, W), BF16),
@@ -365,6 +381,8 @@
             pltpu.VMEM((atoms * TX, cells), F32),
             pltpu.VMEM((sx + TX, cells), F32),
             pltpu.VMEM((TX, cells), F32),
+            pltpu.VMEM((Q, MH, LANES), BF16),
+            dma((Q + 1,)),
             dma((C, C.bit_length())),
             dma((C,)),
             dma((Q, R)),
@@ -388,6 +406,14 @@
             collective_id=0, has_side_effects=True, vmem_limit_bytes=VMEM_MIB * 1024 * 1024
         ),
     )(hamiltonian, density, ham_pattern.T, den_pattern, tile_basis, offsets)
+    return pl.pallas_call(
+        hand_on,
+        out_shape=tuple(jax.ShapeDtypeStruct(x.shape, x.dtype) for x in results),
+        in_specs=[hbm, hbm],
+        out_specs=(hbm, hbm),
+        scratch_shapes=[dma((2,))],
+        compiler_params=pltpu.CompilerParams(vmem_limit_bytes=VMEM_MIB * 1024 * 1024),
+    )(*results)
 
 
 def solution(mesh):

time: 44.2 us -> 43.5 us (0.984)
  local copies, waits for them, and re-layouts: 2.28 us -> 0 us
  Pallas kernels: 41.1 us -> 42.7 us
    pallas_call x0 -> x1, Pallas kernels: none -> 9.56 us  [shards(): pl.pallas_call(hand_on, out_shape=tuple((jax.ShapeDtypeStruct(x.shape, x....]
    pallas_call x1, Pallas kernels: 41.1 us -> 33.1 us  [shards(): pl.pallas_call(functools.partial(kernel, R, C), out_shape=(jax.ShapeDtype...]
    unnamed x4 -> x0, local copies, waits for them, and re-layouts: 2.28 us -> none
where the time goes in v3:
time: 43.5 us; the launch traced here: 43.3 us
  Pallas kernels  42.7 us (98%)
  between operations  0.64 us (1%)
    pallas_call x1, Pallas kernels, shards(): pl.pallas_call(functools.partial(kernel, R, C), out_shape=(jax.ShapeDtype...  33.1 us
    pallas_call x1, Pallas kernels, shards(): pl.pallas_call(hand_on, out_shape=tuple((jax.ShapeDtypeStruct(x.shape, x....  9.56 us

profile of v3, /device:TPU:0, one launch (start us, length us, event | category | flops | bytes accessed | tf_op | source)
XLA Modules:
  0.0 43.3 jit_solution(13581265435961937184)
XLA Ops:
  0.6 33.1 %shard_map.77 = (bf16[256,512]{1,0:T(8,128)(2,1)}, f32[32,128]{1,0:T(8,128)}) custom-call(bf16[512,256]{1,0:T(8,128)(2,1)} %ham_in.1, bf16[256,512]{1,0:T(8,128)(2,1)} %den_in.1, s32[4,8]{1,0:T(4,128)} %bitcast.1, s32[4,8]{1,0:T(4,128)} %dpat_in.1, bf16[64,16,128]{2,1,0:T(8,128)(2,1)} %basis_in.1, s32[4]{0:T(128)} %offsets_in.1), custom_call_target="tpu_custom_call" | custom-call | tf_op jit(solution)/shard_map/pallas_call | solution.py:358
  33.7 9.6 %shard_map.78 = (bf16[256,512]{1,0:T(8,128)(2,1)}, f32[32,128]{1,0:T(8,128)}) custom-call(bf16[256,512]{1,0:T(8,128)(2,1)} %get-tuple-element.4.product, f32[32,128]{1,0:T(8,128)} %get-tuple-element.5.planes), custom_call_target="tpu_custom_call" | custom-call | tf_op jit(solution)/shard_map/pallas_call | solution.py:409

commit v4 on v3

--- a/solution.py
+++ b/solution.py
@@ -11,7 +11,7 @@
 MESH = pl.DeviceIdType.MESH
 TX = 16
 LANES = 128
-VMEM_MIB = 63
+VMEM_KIB = 65536 - 512
 F32 = jnp.float32
 BF16 = jnp.bfloat16
 NT = (((1,), (1,)), ((), ()))
@@ -41,7 +41,7 @@
 def kernel(
     R, C, ham_in, den_in, hpat_in, dpat_in, basis_in, offsets_in, out, grid,
     ham, den, hpat, dpat, basis, offsets,
-    hbuf, dbuf, psend, pown, precv, ssend, srecv, srow, tbuf, trecv, chcol, tiles, ext, incoming, done, stored,
+    hbuf, dbuf, psend, pown, precv, ssend, srecv, srow, tbuf, trecv, chcol, tiles, ext, incoming,
     hs, hr, drs, drr, dls, dlr, xs, xr, cs, cr, ws, wr, ts, tr, gs, gr, loaded, hello,
 ):
     r, c, p = lax.axis_index("row"), lax.axis_index("col"), lax.axis_index("rep")
@@ -265,8 +265,8 @@
 
     def finish_grid():
         g_copy().wait_recv()
-        ext[:TX, :] = ext[:TX, :] + incoming[...]
-        grid_copy().start()
+        grid[TX:, :] = ext[TX:sx, :]
+        grid[:TX, :] = ext[:TX, :] + incoming[...]
 
     def x_copy(q):
         return remote(psend.at[q], precv.at[q], xs.at[q], xr.at[q], peer)
@@ -283,16 +283,9 @@
         x_copy(q).start()
         pown[q] = half(q, p)
 
-    def out_copy(q):
-        return pltpu.make_async_copy(done.at[q], out.at[:, pl.ds(q * LANES, LANES)], stored.at[q])
-
-    def grid_copy():
-        return pltpu.make_async_copy(ext.at[pl.ds(0, sx), :], grid, stored.at[Q])
-
     def drain(q):
         x_copy(q).wait_recv()
-        done[q] = (pown[q] + precv[q]).astype(BF16)
-        out_copy(q).start()
+        out[:, q * LANES : (q + 1) * LANES] = (pown[q] + precv[q]).astype(BF16)
 
     hooks = {
         (0, 1): [sums_over_chips, meet_partner],
@@ -334,17 +327,6 @@
         row_copy(k).wait_send()
     t_copy().wait_send()
     g_copy().wait_send()
-    for q in range(Q):
-        out_copy(q).wait()
-    grid_copy().wait()
-
-
-def hand_on(product, planes, out, grid, sems):
-    copies = [pltpu.make_async_copy(product, out, sems.at[0]), pltpu.make_async_copy(planes, grid, sems.at[1])]
-    for copy in copies:
-        copy.start()
-    for copy in copies:
-        copy.wait()
 
 
 def shards(R, C, hamiltonian, density, ham_pattern, den_pattern, tile_basis, offsets):
@@ -355,11 +337,12 @@
     sx = 32
     dma = pltpu.SemaphoreType.DMA
     hbm = pl.BlockSpec(memory_space=pltpu.HBM)
-    results = pl.pallas_call(
+    vmem = pl.BlockSpec(memory_space=pltpu.VMEM)
+    return pl.pallas_call(
         functools.partial(kernel, R, C),
         out_shape=(jax.ShapeDtypeStruct((MH, W), BF16), jax.ShapeDtypeStruct((sx, cells), F32)),
         in_specs=[hbm] * 6,
-        out_specs=(hbm, hbm),
+        out_specs=(vmem, vmem),
         scratch_shapes=[
             pltpu.VMEM((MR, KH), BF16),
             pltpu.VMEM((KD, W), BF16),
@@ -381,8 +364,6 @@
             pltpu.VMEM((atoms * TX, cells), F32),
             pltpu.VMEM((sx + TX, cells), F32),
             pltpu.VMEM((TX, cells), F32),
-            pltpu.VMEM((Q, MH, LANES), BF16),
-            dma((Q + 1,)),
             dma((C, C.bit_length())),
             dma((C,)),
             dma((Q, R)),
@@ -403,17 +384,9 @@
             pltpu.SemaphoreType.REGULAR,
         ],
         compiler_params=pltpu.CompilerParams(
-            collective_id=0, has_side_effects=True, vmem_limit_bytes=VMEM_MIB * 1024 * 1024
+            collective_id=0, has_side_effects=True, vmem_limit_bytes=VMEM_KIB * 1024
         ),
     )(hamiltonian, density, ham_pattern.T, den_pattern, tile_basis, offsets)
-    return pl.pallas_call(
-        hand_on,
-        out_shape=tuple(jax.ShapeDtypeStruct(x.shape, x.dtype) for x in results),
-        in_specs=[hbm, hbm],
-        out_specs=(hbm, hbm),
-        scratch_shapes=[dma((2,))],
-        compiler_params=pltpu.CompilerParams(vmem_limit_bytes=VMEM_MIB * 1024 * 1024),
-    )(*results)
 
 
 def solution(mesh):

time: 43.5 us -> 36.3 us (0.83)
  Pallas kernels: 42.7 us -> 33.2 us
  local copies, waits for them, and re-layouts: 0 us -> 2.28 us
    pallas_call x1 -> x0, Pallas kernels: 9.56 us -> none  [shards(): pl.pallas_call(hand_on, out_shape=tuple((jax.ShapeDtypeStruct(x.shape, x....]
    unnamed x0 -> x4, local copies, waits for them, and re-layouts: none -> 2.28 us
where the time goes in v4:
time: 36.3 us; the launch traced here: 36.1 us
  Pallas kernels  33.2 us (91%)
  local copies, waits for them, and re-layouts  2.28 us (6%)
  between operations  0.65 us (2%)
    pallas_call x1, Pallas kernels, shards(): pl.pallas_call(functools.partial(kernel, R, C), out_shape=(jax.ShapeDtype...  33.2 us
    unnamed x4, local copies, waits for them, and re-layouts  2.28 us

profile of v4, /device:TPU:0, one launch (start us, length us, event | category | flops | bytes accessed | tf_op | source)
XLA Modules:
  0.0 36.1 jit_solution(15355422327189893939)
XLA Ops:
  0.6 33.2 %shard_map.77 = (bf16[256,512]{1,0:T(8,128)(2,1)}, f32[32,128]{1,0:T(8,128)}) custom-call(bf16[512,256]{1,0:T(8,128)(2,1)} %ham_in.1, bf16[256,512]{1,0:T(8,128)(2,1)} %den_in.1, s32[4,8]{1,0:T(4,128)} %bitcast.1, s32[4,8]{1,0:T(4,128)} %dpat_in.1, bf16[64,16,128]{2,1,0:T(8,128)(2,1)} %basis_in.1, s32[4]{0:T(128)} %offsets_in.1), custom_call_target="tpu_custom_call" | custom-call | tf_op jit(solution)/shard_map/pallas_call | solution.py:341
  33.8 0.0 copy-start
  33.8 1.7 %copy.10 = bf16[256,512]{1,0:T(8,128)(2,1)} copy(bf16[256,512]{1,0:T(8,128)(2,1)} %get-tuple-element.4) | data formatting | bytes 524288
  35.5 0.0 copy-done
  35.5 0.6 %copy.11 = f32[32,128]{1,0:T(8,128)} copy(f32[32,128]{1,0:T(8,128)S(1)} %copy-done) | data formatting | bytes 32768
Async XLA Ops:
  33.8 1.7 %copy-start = (f32[32,128]{1,0:T(8,128)S(1)}, f32[32,128]{1,0:T(8,128)}, u32[]{:S(2)}) copy-start(f32[32,128]{1,0:T(8,128)} %get-tuple-element.5) | copy-start | bytes 49156
